TPU v7x, 32 devices: a whole 2x2x4 slice. The times are simulated.
32 devices in a mesh: runs: 2 (over x), tm: 8 (over z, y), hyd: 2 (over core).
Axes of the slice: x: 2, y: 2, z: 4, core: 2. Of those that a mesh axis runs over, the one named last changes fastest.
Arguments:
- record: bfloat16 [524160, 1024], P(('runs', 'tm'), 'hyd'), parts along dimension 0, may hold values from -6 to 6
- chips: int32 [4095], replicated, may hold values from -1 to 1, as said below
- steer_lags: int32 [1024, 256], P('hyd'), may hold values from 0 to 7
Outputs:
- power: float32 [128, 512, 256], P('runs', 'tm', 'hyd'), parts along dimension 0
There are 2 independent parts, one for each index of `runs`. A program takes and returns all parts, laid end to end along the dimension named above; an argument that names none is the same for every part. Nothing has to cross between parts.
Inputs may be any that keep to these rules, and one draw needn't show every extreme that they name: The chips are +1 or -1 and form one period of a maximal-length sequence of period 4095, starting at a drawn phase.
All inputs are finite; a program needn't handle non-finite values.
Results may differ from a plain program's by a relative error of at most 0.0047.
Values may be sent and summed in bfloat16 or wider, within the bound.
A program may use at most 256 MiB of HBM per device.

v0:
```python
import math
import jax
import jax.numpy as jnp
from jax import lax
from jax.sharding import PartitionSpec as P

CODE = 4095
HYDRO = 1024
DELAYS = 512
PERIODS = 64
BEAMS = 256
MAXLAG = 8


def passed_along(array, axis, by):
    length = lax.axis_size(axis)
    pairs = [(i, i + by) for i in range(length) if 0 <= i + by < length]
    return lax.ppermute(array, axis, pairs)


def toeplitz_code(chips):
    seg_len = CODE + DELAYS - 1
    padded = jnp.concatenate([chips.astype(jnp.float32), jnp.zeros((DELAYS,), jnp.float32)])
    tiled = jnp.tile(padded, DELAYS)[: DELAYS * seg_len]
    return tiled.reshape(DELAYS, seg_len).astype(jnp.bfloat16)


def dft_table(length):
    freq = jnp.arange(length, dtype=jnp.int32)
    phase = (freq[:, None] * freq[None, :] % length).astype(jnp.float32) * (2.0 * math.pi / length)
    weight = 1.0 / math.sqrt(length)
    return jnp.concatenate([jnp.cos(phase) * weight, -jnp.sin(phase) * weight], 0).astype(
        jnp.bfloat16
    )


def body(record, chips, steer_lags):
    hyd_local = record.shape[1]
    tm_size = lax.axis_size("tm")
    local_periods = PERIODS // tm_size
    delay_rows = DELAYS // tm_size
    seg_len = CODE + DELAYS - 1
    norm_code = 1.0 / math.sqrt(CODE)
    tail_rows = passed_along(record[: DELAYS - 1], "tm", -1)
    extended = jnp.concatenate([record, tail_rows], 0)
    toeplitz = toeplitz_code(chips)
    profile_list = []
    for period in range(local_periods):
        segment = extended[period * CODE : period * CODE + seg_len]
        profile_list.append(
            (jnp.dot(toeplitz, segment, preferred_element_type=jnp.float32) * norm_code).astype(
                jnp.bfloat16
            )
        )
    profiles = jnp.stack(profile_list, 0)
    transform = dft_table(PERIODS)
    received = lax.all_to_all(profiles, "tm", split_axis=1, concat_axis=0, tiled=True)
    trailing = received.shape[1:]
    flattened = received.reshape(received.shape[0], -1)
    spectral = jnp.dot(transform, flattened, preferred_element_type=jnp.float32).astype(
        jnp.bfloat16
    )
    spectrum = spectral.reshape((2, received.shape[0]) + trailing)
    next_rows = passed_along(spectrum[:, :, : MAXLAG - 1, :], "tm", -1)
    spec_ext = jnp.concatenate([spectrum, next_rows], 2)
    norm_hydro = 1.0 / math.sqrt(HYDRO)
    shifted_list = [
        spec_ext[:, :, offset : offset + delay_rows, :].reshape(2 * PERIODS * delay_rows, hyd_local)
        for offset in range(MAXLAG)
    ]
    beam_local = BEAMS // lax.axis_size("hyd")
    partial_sum = jnp.zeros((2 * PERIODS * delay_rows, BEAMS), jnp.float32)
    for offset in range(MAXLAG):
        selector = (steer_lags == offset).astype(jnp.bfloat16)
        partial_sum = partial_sum + jnp.dot(
            shifted_list[offset], selector, preferred_element_type=jnp.float32
        )
    summed = lax.psum(partial_sum * norm_hydro, "hyd")
    owned = lax.dynamic_slice_in_dim(summed, lax.axis_index("hyd") * beam_local, beam_local, 1)
    owned = owned.reshape(2, PERIODS, delay_rows, beam_local)
    return owned[0] * owned[0] + owned[1] * owned[1]


def solution(mesh):
    in_specs = (P(("runs", "tm"), "hyd"), P(), P("hyd", None))
    out_specs = P("runs", "tm", "hyd")
    return jax.shard_map(body, mesh=mesh, in_specs=in_specs, out_specs=out_specs, check_vma=False)
```

profile of v0, /device:TPU:0, one launch (start us, length us, event | category | flops | bytes accessed | tf_op | source)
XLA Modules:
  0.0 408.6 jit_solution(9783359401931948476)
XLA Ops:
  6.5 1.1 slice.73
  7.6 1.3 collective-permute-start
  8.9 0.7 convert_element_type.49
  9.6 2.5 tile.10
  12.1 11.8 %tile.11 = bf16[2358784]{0:T(1024)(128)(2,1)} reshape(bf16[512,4607]{1,0:T(8,128)(2,1)} %tile.10) | data formatting | bytes 9435136 | tf_op jit(solution)/shard_map/tile | solution.py:24
  23.9 5.7 %slice.85 = bf16[2358272]{0:T(1024)(128)(2,1)} slice(bf16[2358784]{0:T(1024)(128)(2,1)} %tile.11), slice={[0:2358272]} | slice | bytes 9433088 | tf_op jit(solution)/shard_map/slice | solution.py:24
  29.6 11.3 %convert_element_type.50 = bf16[512,4606]{1,0:T(8,128)(2,1)} reshape(bf16[2358272]{0:T(1024)(128)(2,1)} %slice.85) | data formatting | bytes 9433088 | tf_op jit(solution)/shard_map/convert_element_type | solution.py:25
  40.9 7.3 %fusion.65 = bf16[8,512,512]{2,1,0:T(8,128)(2,1)} fusion(bf16[512,4606]{1,0:T(8,128)(2,1)} %convert_element_type.50, bf16[32760,512]{1,0:T(8,128)(2,1)} %param.3), kind=kOutput, calls=%fused_computation.47 | convolution fusion | flops 2415394816 | bytes 9961472 | tf_op jit(solution)/shard_map/dot_general | solution.py:51
  48.2 0.0 copy-done.1
  48.2 0.0 slice-start.2
  48.2 0.0 slice-start.3
  48.2 0.0 slice-start.4
  48.3 0.0 slice-start.5
  48.3 0.0 slice-start.6
  48.3 5.9 %fusion.73 = bf16[8,512,512]{2,1,0:T(8,128)(2,1)} fusion(bf16[8,512,512]{2,1,0:T(8,128)(2,1)} %fusion.65, bf16[512,4606]{1,0:T(8,128)(2,1)S(1)} %copy-done.1, bf16[32760,512]{1,0:T(8,128)(2,1)} %param.3), kind=kOutput, calls=%fused_computation.51 | convolution fusion | flops 2415394816 | bytes 9959424 | tf_op jit(solution)/shard_map/dot_general | solution.py:51
  54.2 0.0 slice-start.7
  54.2 6.6 %fusion.79 = bf16[8,512,512]{2,1,0:T(8,128)(2,1)} fusion(bf16[8,512,512]{2,1,0:T(8,128)(2,1)} %fusion.73, bf16[512,4606]{1,0:T(8,128)(2,1)S(1)} %copy-done.1, bf16[32760,512]{1,0:T(8,128)(2,1)} %param.3), kind=kOutput, calls=%fused_computation.53 | convolution fusion | flops 2415394816 | bytes 9959424 | tf_op jit(solution)/shard_map/dot_general | solution.py:51
  60.8 0.0 slice-done.2
  60.8 0.0 slice-done.3
  60.8 0.0 slice-done.4
  60.8 0.0 slice-done.5
  60.8 0.0 slice-done.6
  60.9 0.0 slice-done.7
  60.9 0.0 slice-done.8
  60.9 1.4 slice-done.9
  62.3 3.7 fusion.85
  66.0 3.5 fusion.91
  69.5 3.5 fusion.97
  73.0 3.5 fusion.103
  76.5 0.0 collective-permute-done
  76.5 5.9 %fusion.69 = bf16[8,512,512]{2,1,0:T(8,128)(2,1)} fusion(bf16[8,512,512]{2,1,0:T(8,128)(2,1)} %fusion.103, bf16[512,4606]{1,0:T(8,128)(2,1)} %convert_element_type.50, bf16[511,512]{1,0:T(8,128)(2,1)S(1)} %collective-permute-done, bf16[32760,512]{1,0:T(8,128)(2,1)S(1)} %bitcast.82), kind=kOutput, calls=%fused_computation.49 | convolution fusion | flops 2424827904 | bytes 39312384 | tf_op jit(solution)/shard_map/dot_general | solution.py:51
  82.5 6.9 %copy.5 = bf16[8,512,512]{2,0,1:T(8,128)(2,1)} copy(bf16[8,512,512]{2,1,0:T(8,128)(2,1)} %fusion.69) | data formatting | bytes 8388608 | tf_op jit(solution)/shard_map/stack | solution.py:55
  89.3 8.4 %all-to-all-start = ((bf16[8,512,512]{2,0,1:T(8,128)(2,1)}), bf16[8,512,512]{2,0,1:T(8,128)(2,1)}, u32[]{:S(2)}, u32[]{:S(2)}) async-start(bf16[8,512,512]{2,0,1:T(8,128)(2,1)} %copy.5), calls=%async_computation | async-start | bytes 8388608 | tf_op jit(solution)/shard_map/all_to_all | solution.py:57
  97.8 0.0 all-reduce.3.cloned.1.call-start
  97.8 0.2 multiply_convert_fusion
  98.0 92.8 %all-to-all-done = bf16[8,512,512]{2,0,1:T(8,128)(2,1)} async-done(((bf16[8,512,512]{2,0,1:T(8,128)(2,1)}), bf16[8,512,512]{2,0,1:T(8,128)(2,1)}, u32[]{:S(2)}, u32[]{:S(2)}) %all-to-all-start) | async-done | bytes 4194336 | tf_op jit(solution)/shard_map/all_to_all | solution.py:57
  190.8 3.8 copy.14
  194.6 2.6 copy.10
  197.1 5.6 %convolution_convert_fusion = bf16[128,32768]{1,0:T(8,128)(2,1)} fusion(bf16[64,32768]{1,0:T(8,128)(2,1)S(1)} %bitcast.83, bf16[64,64]{1,0:T(8,128)(2,1)S(1)} %get-tuple-element.12, bf16[64,64]{1,0:T(8,128)(2,1)S(1)} %get-tuple-element.13), kind=kOutput, calls=%fused_computation | convolution fusion | flops 541097984 | bytes 12599296 | tf_op jit(solution)/shard_map/dot_general | solution.py:60
  202.7 13.6 %reshape_reshape.3 = bf16[8192,512]{1,0:T(8,128)(2,1)} reshape(bf16[128,32768]{1,0:T(8,128)(2,1)} %convolution_convert_fusion) | data formatting | bytes 16777216 | tf_op jit(solution)/shard_map/reshape;reshape | solution.py:68
  216.3 10.2 %copy.11 = bf16[16,8,64,512]{3,2,1,0:T(8,128)(2,1)} copy(bf16[16,8,64,512]{3,1,2,0:T(8,128)(2,1)} %bitcast.69) | data formatting | bytes 16777216
  226.6 8.0 %constant_dynamic-update-slice_fusion = bf16[2,64,71,512]{3,2,1,0:T(8,128)(2,1)} fusion(bf16[2,64,64,512]{3,2,1,0:T(8,128)(2,1)} %bitcast.79), kind=kLoop, calls=%fused_computation.94 | loop fusion | bytes 16777216
  234.6 1.3 slice.86
  235.9 0.3 copy.9
  236.2 1.3 collective-permute-start.1
  237.5 0.0 copy-done
  237.5 9.1 %fusion.113 = f32[8192,256]{1,0:T(8,128)} fusion(bf16[8192,512]{1,0:T(8,128)(2,1)} %reshape_reshape.3, s32[512,256]{1,0:T(8,128)S(1)} %copy-done), kind=kOutput, calls=%fused_computation.70 | convolution fusion | flops 2147614720 | bytes 17301504 | tf_op jit(solution)/shard_map/dot_general | solution.py:75
  246.7 12.5 %collective-permute-done.1 = bf16[2,64,7,512]{3,1,2,0:T(8,128)(2,1)S(1)} collective-permute-done((bf16[2,64,7,512]{3,1,2,0:T(8,128)(2,1)S(1)}, bf16[2,64,7,512]{3,1,2,0:T(8,128)(2,1)S(1)}, u32[]{:S(2)}, u32[]{:S(2)}) %collective-permute-start.1) | collective-permute-done | bytes 917536 | tf_op jit(solution)/shard_map/ppermute | solution.py:18
  259.1 1.6 copy_dynamic-update-slice_fusion
  260.7 52.8 %fusion.142 = (bf16[2,64,64,512]{3,2,1,0:T(8,128)(2,1)}, bf16[2,64,64,512]{3,2,1,0:T(8,128)(2,1)}, bf16[2,64,64,512]{3,2,1,0:T(8,128)(2,1)}, bf16[2,64,64,512]{3...) fusion(bf16[2,64,71,512]{3,2,1,0:T(8,128)(2,1)} %copy_dynamic-u, ...), kind=kLoop, calls=%fused_computation.106 | loop fusion | bytes 117440512 | tf_op jit(solution)/shard_map/slice | solution.py:68
  313.6 8.4 %convolution_add_fusion.6 = f32[8192,256]{1,0:T(8,128)S(1)} fusion(f32[8192,256]{1,0:T(8,128)} %fusion.113, bf16[8192,512]{1,0:T(8,128)(2,1)} %bitcast.78, s32[512,256]{1,0:T(8,128)S(1)} %copy-done), kind=kOutput, calls=%fused_computation.8 | convolution fusion | flops 2149711872 | bytes 25690112 | tf_op jit(solution)/shard_map/dot_general | solution.py:75
  322.0 0.0 slice-start
  322.0 6.1 %convolution_add_fusion.5 = f32[8192,256]{1,0:T(8,128)S(1)} fusion(f32[8192,256]{1,0:T(8,128)S(1)} %convolution_add_fusion.6, bf16[8192,512]{1,0:T(8,128)(2,1)} %bitcast.77, s32[512,256]{1,0:T(8,128)S(1)} %copy-done), kind=kOutput, calls=%fused_computation.7 | convolution fusion | flops 2149711872 | bytes 25690112 | tf_op jit(solution)/shard_map/dot_general | solution.py:75
  328.1 0.0 slice-start.1
  328.1 6.1 %convolution_add_fusion.4 = f32[8192,256]{1,0:T(8,128)S(1)} fusion(f32[8192,256]{1,0:T(8,128)S(1)} %convolution_add_fusion.5, bf16[8192,512]{1,0:T(8,128)(2,1)} %bitcast.76, s32[512,256]{1,0:T(8,128)S(1)} %copy-done), kind=kOutput, calls=%fused_computation.6 | convolution fusion | flops 2149711872 | bytes 25690112 | tf_op jit(solution)/shard_map/dot_general | solution.py:75
  334.3 0.0 slice-done
  334.3 0.0 slice-done.1
  334.3 2.4 convolution_add_fusion.3
  336.7 6.3 %convolution_add_fusion.2 = f32[8192,256]{1,0:T(8,128)S(1)} fusion(f32[8192,256]{1,0:T(8,128)S(1)} %convolution_add_fusion.3, bf16[8192,512]{1,0:T(8,128)(2,1)} %bitcast.72, s32[512,256]{1,0:T(8,128)S(1)} %copy-done), kind=kOutput, calls=%fused_computation.4 | convolution fusion | flops 2149711872 | bytes 25690112 | tf_op jit(solution)/shard_map/dot_general | solution.py:75
  343.0 6.0 %convolution_add_fusion.1 = f32[8192,256]{1,0:T(8,128)S(1)} fusion(f32[8192,256]{1,0:T(8,128)S(1)} %convolution_add_fusion.2, bf16[8192,512]{1,0:T(8,128)(2,1)} %bitcast.71, s32[512,256]{1,0:T(8,128)S(1)} %copy-done), kind=kOutput, calls=%fused_computation.3 | convolution fusion | flops 2149711872 | bytes 25690112 | tf_op jit(solution)/shard_map/dot_general | solution.py:75
  349.0 9.2 %fusion = f32[8192,256]{1,0:T(8,128)} fusion(f32[8192,256]{1,0:T(8,128)S(1)} %convolution_add_fusion.1, bf16[8192,512]{1,0:T(8,128)(2,1)} %bitcast.70, s32[512,256]{1,0:T(8,128)S(1)} %copy-done), kind=kOutput, calls=%fused_computation.2 | convolution fusion | flops 2151809024 | bytes 25690112 | tf_op jit(solution)/shard_map/dot_general | solution.py:75
  358.2 0.0 all-reduce.3.cloned.1.call-update
  358.2 39.2 %all-reduce.3.cloned.1.call-done = f32[8192,256]{1,0:T(8,128)} async-done(((f32[8192,256]{1,0:T(8,128)}), f32[8192,256]{1,0:T(8,128)}) %all-reduce.3.cloned.1.call-update) | async-done | bytes 8388624 | tf_op jit(solution)/shard_map/psum | solution.py:78
  397.5 3.8 fusion.17
  (7 shorter events, 0.0 us)
Async XLA Ops:
  7.6 68.9 %collective-permute-start = (bf16[511,512]{1,0:T(8,128)(2,1)S(1)}, bf16[511,512]{1,0:T(8,128)(2,1)S(1)}, u32[]{:S(2)}, u32[]{:S(2)}) collective-permute-start(bf16[511,512]{1,0:T(8,128)(2,1)S(1)} %slice.73), channel_id=1, source_target_pairs={{2,0},{4,2},{6,4},{8,6},{10,8},{12,10},{14,12},{3,1},{5,3},{7,5},{... | collective-permute-start | bytes 1569800 | tf_op jit(solution)/shard_map/ppermute | solution.py:18
  40.9 7.3 %copy-start.1 = (bf16[512,4606]{1,0:T(8,128)(2,1)S(1)}, bf16[512,4606]{1,0:T(8,128)(2,1)}, u32[]{:S(2)}) copy-start(bf16[512,4606]{1,0:T(8,128)(2,1)} %convert_element_type.50) | copy-start | bytes 14149636
  48.2 12.6 %slice-start.2 = ((s8[33546240]{0:T(1024)(128)(4,1)}), s8[4194304]{0:T(1024)(128)(4,1)S(1)}, s32[]{:S(2)}) async-start(s8[33546240]{0:T(1024)(128)(4,1)} %bitcast.81), calls=%async_computation.4 | async-start | bytes 8388608
  48.2 12.6 %slice-start.3 = ((s8[33546240]{0:T(1024)(128)(4,1)}), s8[4194304]{0:T(1024)(128)(4,1)S(1)}, s32[]{:S(2)}) async-start(s8[33546240]{0:T(1024)(128)(4,1)} %bitcast.81), calls=%async_computation.5 | async-start | bytes 8388608
  48.2 12.6 %slice-start.4 = ((s8[33546240]{0:T(1024)(128)(4,1)}), s8[4194304]{0:T(1024)(128)(4,1)S(1)}, s32[]{:S(2)}) async-start(s8[33546240]{0:T(1024)(128)(4,1)} %bitcast.81), calls=%async_computation.6 | async-start | bytes 8388608
  48.3 12.6 %slice-start.5 = ((s8[33546240]{0:T(1024)(128)(4,1)}), s8[4194304]{0:T(1024)(128)(4,1)S(1)}, s32[]{:S(2)}) async-start(s8[33546240]{0:T(1024)(128)(4,1)} %bitcast.81), calls=%async_computation.7 | async-start | bytes 8388608
  48.3 12.6 %slice-start.6 = ((s8[33546240]{0:T(1024)(128)(4,1)}), s8[4194304]{0:T(1024)(128)(4,1)S(1)}, s32[]{:S(2)}) async-start(s8[33546240]{0:T(1024)(128)(4,1)} %bitcast.81), calls=%async_computation.8 | async-start | bytes 8388608
  54.2 6.6 %slice-start.7 = ((s8[33546240]{0:T(1024)(128)(4,1)}), s8[4194304]{0:T(1024)(128)(4,1)S(1)}, s32[]{:S(2)}) async-start(s8[33546240]{0:T(1024)(128)(4,1)} %bitcast.81), calls=%async_computation.9 | async-start | bytes 8388608
  54.2 6.7 %slice-start.8 = ((s8[33546240]{0:T(1024)(128)(4,1)}), s8[4194304]{0:T(1024)(128)(4,1)S(1)}, s32[]{:S(2)}) async-start(s8[33546240]{0:T(1024)(128)(4,1)} %bitcast.81), calls=%async_computation.10 | async-start | bytes 8388608
  54.2 8.0 %slice-start.9 = ((s8[33546240]{0:T(1024)(128)(4,1)}), s8[4186112]{0:T(1024)(128)(4,1)S(1)}, s32[]{:S(2)}) async-start(s8[33546240]{0:T(1024)(128)(4,1)} %bitcast.81), calls=%async_computation.11 | async-start | bytes 8372224
  89.3 101.4 %all-to-all-start = ((bf16[8,512,512]{2,0,1:T(8,128)(2,1)}), bf16[8,512,512]{2,0,1:T(8,128)(2,1)}, u32[]{:S(2)}, u32[]{:S(2)}) async-start(bf16[8,512,512]{2,0,1:T(8,128)(2,1)} %copy.5), calls=%async_computation | async-start | bytes 8388608 | tf_op jit(solution)/shard_map/all_to_all | solution.py:57
  97.8 299.7 %all-reduce.3.cloned.1.call-start = ((), (), s32[]{:S(2)}) async-start(), calls=%async_computation.1 | async-start | bytes 16777216 | tf_op jit(solution)/shard_map/psum | solution.py:78
  226.6 10.9 %copy-start = (s32[512,256]{1,0:T(8,128)S(1)}, s32[512,256]{1,0:T(8,128)}, u32[]{:S(2)}) copy-start(s32[512,256]{1,0:T(8,128)} %param.5) | copy-start | bytes 1572868
  236.2 22.9 %collective-permute-start.1 = (bf16[2,64,7,512]{3,1,2,0:T(8,128)(2,1)S(1)}, bf16[2,64,7,512]{3,1,2,0:T(8,128)(2,1)S(1)}, u32[]{:S(2)}, u32[]{:S(2)}) collective-permute-start(bf16[2,64,7,512]{3,1,2,0:T(8,128)(2,1)S(1)} %copy.9), channel_id=1, source_target_pairs={{2,0},{4,2},{6,4},{8,6},{10,8},{12,10},{14,12},{3,1},{5,3},{7,5},{... | collective-permute-start | bytes 2752520 | tf_op jit(solution)/shard_map/ppermute | solution.py:18
  322.0 12.3 %slice-start = ((s8[8388608]{0:T(1024)(128)(4,1)}), s8[4194304]{0:T(1024)(128)(4,1)S(1)}, s32[]{:S(2)}) async-start(s8[8388608]{0:T(1024)(128)(4,1)} %bitcast.73), calls=%async_computation.2 | async-start | bytes 8388608
  328.1 6.2 %slice-start.1 = ((s8[8388608]{0:T(1024)(128)(4,1)}), s8[4194304]{0:T(1024)(128)(4,1)S(1)}, s32[]{:S(2)}) async-start(s8[8388608]{0:T(1024)(128)(4,1)} %bitcast.73), calls=%async_computation.3 | async-start | bytes 8388608
Sparse Core Ops, SparseCore 0:
  358.3 39.0 all-reduce.2
where the time goes:
time: 416 us; the launch traced here: 409 us
  waiting for transfers between devices  145 us (35%)
  local copies, waits for them, and re-layouts  135 us (32%)
  matrix products  99.3 us (24%)
  between operations  14.1 us (3%)
  starting transfers between devices  11 us (3%)
  other arithmetic  4.64 us (1%)
    all_to_all x1, waiting for transfers between devices, body(): lax.all_to_all(profiles, 'tm', split_axis=1, concat_axis=0, tiled=True)  92.8 us
    dot_general x8, matrix products, body(): jnp.dot(shifted_list[offset], selector, preferred_element_type=jnp.float32)  53.7 us
    slice x1, local copies, waits for them, and re-layouts, body(): spec_ext[:, :, offset:offset + delay_rows, :]  52.8 us
    dot_general x8, matrix products, body(): jnp.dot(toeplitz, segment, preferred_element_type=jnp.float32) * norm_code  40 us
    psum x1, waiting for transfers between devices, body(): summed = lax.psum(partial_sum * norm_hydro, 'hyd')  39.2 us
    unnamed x28, local copies, waits for them, and re-layouts  22.6 us
    another operation x2, local copies, waits for them, and re-layouts, toeplitz_code(): tiled = jnp.tile(padded, DELAYS)[:DELAYS * seg_len]  14.3 us
    another operation x1, local copies, waits for them, and re-layouts, body(): spec_ext[:, :, offset:offset + delay_rows, :]  13.6 us
  transfers between devices with their start and end apart: 4, of which 3 were waited for; matrix products, arithmetic and copies ran while one was open for 18% of the time, Pallas kernels for 0%

commit v1 on v0

--- a/solution.py
+++ b/solution.py
@@ -10,6 +10,13 @@
 PERIODS = 64
 BEAMS = 256
 MAXLAG = 8
+
+
+def trade_parts(x, axis, split, join):
+    peers = lax.axis_size(axis)
+    blocks = jnp.stack(jnp.split(x, peers, axis=split), axis=0)
+    blocks = lax.all_to_all(blocks, axis, split_axis=0, concat_axis=0)
+    return jnp.concatenate(blocks, axis=join)
 
 
 def passed_along(array, axis, by):
@@ -54,7 +61,7 @@
         )
     profiles = jnp.stack(profile_list, 0)
     transform = dft_table(PERIODS)
-    received = lax.all_to_all(profiles, "tm", split_axis=1, concat_axis=0, tiled=True)
+    received = trade_parts(profiles, "tm", 1, 0)
     trailing = received.shape[1:]
     flattened = received.reshape(received.shape[0], -1)
     spectral = jnp.dot(transform, flattened, preferred_element_type=jnp.float32).astype(

time: 416 us -> 415 us (level)
  matrix products: 99.3 us -> 92 us
  local copies, waits for them, and re-layouts: 135 us -> 142 us
    unnamed x28 -> x43, local copies, waits for them, and re-layouts: 22.6 us -> 37.8 us
    dot_general x8, matrix products: 53.7 us -> 46.4 us  [body(): jnp.dot(shifted_list[offset], selector, preferred_element_type=jnp.float32)]
    another operation x2, local copies, waits for them, and re-layouts: 6.88 us -> 1.92 us  [the longest x1 1.91 us: trade_parts(): blocks = jnp.stack(jnp.split(x, peers, axis=split), axis=0)]
  transfers between devices with their start and end apart: 4 -> 4, of which waited for: 3 -> 3; matrix products, arithmetic and copies ran while one was open for 18% -> 19% of each run, Pallas kernels for 0% -> 0%
where the time goes in v1:
time: 415 us; the launch traced here: 408 us
  waiting for transfers between devices  144 us (35%)
  local copies, waits for them, and re-layouts  142 us (34%)
  matrix products  92 us (22%)
  between operations  13.9 us (3%)
  starting transfers between devices  11.7 us (3%)
  other arithmetic  4.64 us (1%)
    all_to_all x1, waiting for transfers between devices, trade_parts(): blocks = lax.all_to_all(blocks, axis, split_axis=0, concat_axis=0)  92.6 us
    slice x1, local copies, waits for them, and re-layouts, body(): spec_ext[:, :, offset:offset + delay_rows, :]  53 us
    dot_general x8, matrix products, body(): jnp.dot(shifted_list[offset], selector, preferred_element_type=jnp.float32)  46.4 us
    dot_general x8, matrix products, body(): jnp.dot(toeplitz, segment, preferred_element_type=jnp.float32) * norm_code  39.9 us
    psum x1, waiting for transfers between devices, body(): summed = lax.psum(partial_sum * norm_hydro, 'hyd')  39.2 us
    unnamed x43, local copies, waits for them, and re-layouts  37.8 us
    another operation x2, local copies, waits for them, and re-layouts, toeplitz_code(): tiled = jnp.tile(padded, DELAYS)[:DELAYS * seg_len]  14.3 us
    another operation x1, local copies, waits for them, and re-layouts, body(): spec_ext[:, :, offset:offset + delay_rows, :]  13.5 us
  transfers between devices with their start and end apart: 4, of which 3 were waited for; matrix products, arithmetic and copies ran while one was open for 19% of the time, Pallas kernels for 0%

profile of v1, /device:TPU:0, one launch (start us, length us, event | category | flops | bytes accessed | tf_op | source)
XLA Modules:
  0.0 407.7 jit_solution(14679334907386854929)
XLA Ops:
  6.5 1.1 slice.73
  7.6 1.3 collective-permute-start
  8.9 0.7 convert_element_type.49
  9.6 2.5 tile.10
  12.1 11.8 %tile.11 = bf16[2358784]{0:T(1024)(128)(2,1)} reshape(bf16[512,4607]{1,0:T(8,128)(2,1)} %tile.10) | data formatting | bytes 9435136 | tf_op jit(solution)/shard_map/tile | solution.py:31
  23.9 5.9 %slice.85 = bf16[2358272]{0:T(1024)(128)(2,1)} slice(bf16[2358784]{0:T(1024)(128)(2,1)} %tile.11), slice={[0:2358272]} | slice | bytes 9433088 | tf_op jit(solution)/shard_map/slice | solution.py:31
  29.8 11.3 %convert_element_type.50 = bf16[512,4606]{1,0:T(8,128)(2,1)} reshape(bf16[2358272]{0:T(1024)(128)(2,1)} %slice.85) | data formatting | bytes 9433088 | tf_op jit(solution)/shard_map/convert_element_type | solution.py:32
  41.2 7.3 %fusion.65 = bf16[8,512,512]{2,1,0:T(8,128)(2,1)} fusion(bf16[512,4606]{1,0:T(8,128)(2,1)} %convert_element_type.50, bf16[32760,512]{1,0:T(8,128)(2,1)} %param.3), kind=kOutput, calls=%fused_computation.46 | convolution fusion | flops 2415394816 | bytes 9961472 | tf_op jit(solution)/shard_map/dot_general | solution.py:58
  48.5 0.0 slice-start.9
  48.5 0.0 slice-start.10
  48.5 5.9 %fusion.73 = bf16[8,512,512]{2,1,0:T(8,128)(2,1)} fusion(bf16[8,512,512]{2,1,0:T(8,128)(2,1)} %fusion.65, bf16[512,4606]{1,0:T(8,128)(2,1)S(1)} %copy-done.1, bf16[32760,512]{1,0:T(8,128)(2,1)} %param.3), kind=kOutput, calls=%fused_computation.50 | convolution fusion | flops 2415394816 | bytes 9959424 | tf_op jit(solution)/shard_map/dot_general | solution.py:58
  54.5 6.6 %fusion.79 = bf16[8,512,512]{2,1,0:T(8,128)(2,1)} fusion(bf16[8,512,512]{2,1,0:T(8,128)(2,1)} %fusion.73, bf16[512,4606]{1,0:T(8,128)(2,1)S(1)} %copy-done.1, bf16[32760,512]{1,0:T(8,128)(2,1)} %param.3), kind=kOutput, calls=%fused_computation.52 | convolution fusion | flops 2415394816 | bytes 9959424 | tf_op jit(solution)/shard_map/dot_general | solution.py:58
  61.1 0.0 slice-done.9
  61.1 0.0 slice-done.10
  61.1 0.0 slice-done.11
  61.1 0.1 slice-done.12
  61.1 1.4 slice-done.13
  62.5 3.7 fusion.85
  66.2 3.5 fusion.91
  69.7 3.5 fusion.97
  73.2 3.5 fusion.103
  76.7 0.0 collective-permute-done
  76.7 5.9 %fusion.69 = bf16[8,512,512]{2,1,0:T(8,128)(2,1)} fusion(bf16[8,512,512]{2,1,0:T(8,128)(2,1)} %fusion.103, bf16[512,4606]{1,0:T(8,128)(2,1)} %convert_element_type.50, bf16[511,512]{1,0:T(8,128)(2,1)S(1)} %collective-permute-done, bf16[32760,512]{1,0:T(8,128)(2,1)S(1)} %bitcast.114), kind=kOutput, calls=%fused_computation.48 | convolution fusion | flops 2424827904 | bytes 39312384 | tf_op jit(solution)/shard_map/dot_general | solution.py:58
  82.6 1.9 fusion.113
  84.5 1.9 fusion.112
  86.3 1.9 fusion.111
  88.2 1.9 fusion.110
  90.1 1.9 fusion.109
  91.9 1.9 fusion.108
  93.8 1.9 fusion.107
  95.7 1.9 fusion.106
  97.6 8.4 %all-to-all-start = ((bf16[8,8,64,512]{3,2,1,0:T(8,128)(2,1)}), bf16[8,8,64,512]{3,2,1,0:T(8,128)(2,1)}, u32[]{:S(2)}, u32[]{:S(2)}) async-start(bf16[8,8,64,512]{3,2,1,0:T(8,128)(2,1)} %fusion.106), calls=%async_computation | async-start | bytes 8388608 | tf_op jit(solution)/shard_map/all_to_all | solution.py:18
  106.0 0.2 all-reduce.3.cloned.1.call-start
  106.3 0.2 multiply_convert_fusion
  106.4 92.6 %all-to-all-done = bf16[8,8,64,512]{3,2,1,0:T(8,128)(2,1)} async-done(((bf16[8,8,64,512]{3,2,1,0:T(8,128)(2,1)}), bf16[8,8,64,512]{3,2,1,0:T(8,128)(2,1)}, u32[]{:S(2)}, u32[]{:S(2)}) %all-to-all-start) | async-done | bytes 4194336 | tf_op jit(solution)/shard_map/all_to_all | solution.py:18
  199.0 4.7 %copy.7 = bf16[8,8,64,512]{3,1,2,0:T(8,128)(2,1)S(1)} copy(bf16[8,8,64,512]{3,2,1,0:T(8,128)(2,1)} %all-to-all-done) | data formatting | bytes 8388608
  203.8 5.6 %convolution_convert_fusion = bf16[128,32768]{1,0:T(8,128)(2,1)} fusion(bf16[64,32768]{1,0:T(8,128)(2,1)S(1)} %bitcast.115, bf16[64,64]{1,0:T(8,128)(2,1)S(1)} %get-tuple-element.12, bf16[64,64]{1,0:T(8,128)(2,1)S(1)} %get-tuple-element.13), kind=kOutput, calls=%fused_computation | convolution fusion | flops 541097984 | bytes 12599296 | tf_op jit(solution)/shard_map/dot_general | solution.py:67
  209.4 13.5 %reshape_reshape.7 = bf16[8192,512]{1,0:T(8,128)(2,1)} reshape(bf16[128,32768]{1,0:T(8,128)(2,1)} %convolution_convert_fusion) | data formatting | bytes 16777216 | tf_op jit(solution)/shard_map/reshape;reshape | solution.py:75
  222.8 10.2 %copy.8 = bf16[16,8,64,512]{3,2,1,0:T(8,128)(2,1)} copy(bf16[16,8,64,512]{3,1,2,0:T(8,128)(2,1)} %bitcast.97) | data formatting | bytes 16777216
  233.1 8.0 %constant_dynamic-update-slice_fusion = bf16[2,64,71,512]{3,2,1,0:T(8,128)(2,1)} fusion(bf16[2,64,64,512]{3,2,1,0:T(8,128)(2,1)} %bitcast.111), kind=kLoop, calls=%fused_computation.98 | loop fusion | bytes 16777216
  241.0 1.3 slice.86
  242.3 0.3 copy.6
  242.6 1.7 collective-permute-start.1
  244.3 0.0 copy-done
  244.4 9.1 %fusion.121 = f32[8192,256]{1,0:T(8,128)} fusion(bf16[8192,512]{1,0:T(8,128)(2,1)} %reshape_reshape.7, s32[512,256]{1,0:T(8,128)S(1)} %copy-done), kind=kOutput, calls=%fused_computation.85 | convolution fusion | flops 2147614720 | bytes 17301504 | tf_op jit(solution)/shard_map/dot_general | solution.py:82
  253.5 12.1 %collective-permute-done.1 = bf16[2,64,7,512]{3,1,2,0:T(8,128)(2,1)S(1)} collective-permute-done((bf16[2,64,7,512]{3,1,2,0:T(8,128)(2,1)S(1)}, bf16[2,64,7,512]{3,1,2,0:T(8,128)(2,1)S(1)}, u32[]{:S(2)}, u32[]{:S(2)}) %collective-permute-start.1) | collective-permute-done | bytes 917536 | tf_op jit(solution)/shard_map/ppermute | solution.py:25
  265.6 1.5 copy_dynamic-update-slice_fusion
  267.1 53.0 %fusion.150 = (bf16[2,64,64,512]{3,2,1,0:T(8,128)(2,1)}, bf16[2,64,64,512]{3,2,1,0:T(8,128)(2,1)}, bf16[2,64,64,512]{3,2,1,0:T(8,128)(2,1)}, bf16[2,64,64,512]{3...) fusion(bf16[2,64,71,512]{3,2,1,0:T(8,128)(2,1)} %copy_dynamic-u, ...), kind=kLoop, calls=%fused_computation.121 | loop fusion | bytes 117440512 | tf_op jit(solution)/shard_map/slice | solution.py:75
  320.1 0.0 slice-start.4
  320.1 0.0 slice-start.5
  320.1 8.4 %convolution_add_fusion.6 = f32[8192,256]{1,0:T(8,128)S(1)} fusion(f32[8192,256]{1,0:T(8,128)} %fusion.121, bf16[8192,512]{1,0:T(8,128)(2,1)} %bitcast.110, s32[512,256]{1,0:T(8,128)S(1)} %copy-done), kind=kOutput, calls=%fused_computation.8 | convolution fusion | flops 2149711872 | bytes 25690112 | tf_op jit(solution)/shard_map/dot_general | solution.py:82
  328.6 2.4 convolution_add_fusion.5
  331.0 0.0 slice-start.2
  331.0 0.0 slice-start.3
  331.0 6.1 %convolution_add_fusion.4 = f32[8192,256]{1,0:T(8,128)S(1)} fusion(f32[8192,256]{1,0:T(8,128)S(1)} %convolution_add_fusion.5, bf16[8192,512]{1,0:T(8,128)(2,1)} %bitcast.106, s32[512,256]{1,0:T(8,128)S(1)} %copy-done), kind=kOutput, calls=%fused_computation.6 | convolution fusion | flops 2149711872 | bytes 25690112 | tf_op jit(solution)/shard_map/dot_general | solution.py:82
  337.2 2.4 convolution_add_fusion.3
  339.6 6.2 %convolution_add_fusion.2 = f32[8192,256]{1,0:T(8,128)S(1)} fusion(f32[8192,256]{1,0:T(8,128)S(1)} %convolution_add_fusion.3, bf16[8192,512]{1,0:T(8,128)(2,1)} %bitcast.102, s32[512,256]{1,0:T(8,128)S(1)} %copy-done), kind=kOutput, calls=%fused_computation.4 | convolution fusion | flops 2149711872 | bytes 25690112 | tf_op jit(solution)/shard_map/dot_general | solution.py:82
  345.8 0.0 slice-start
  345.8 0.0 slice-start.1
  345.8 6.1 %convolution_add_fusion.1 = f32[8192,256]{1,0:T(8,128)S(1)} fusion(f32[8192,256]{1,0:T(8,128)S(1)} %convolution_add_fusion.2, bf16[8192,512]{1,0:T(8,128)(2,1)} %bitcast.101, s32[512,256]{1,0:T(8,128)S(1)} %copy-done), kind=kOutput, calls=%fused_computation.3 | convolution fusion | flops 2149711872 | bytes 25690112 | tf_op jit(solution)/shard_map/dot_general | solution.py:82
  352.0 5.7 %fusion = f32[8192,256]{1,0:T(8,128)} fusion(f32[8192,256]{1,0:T(8,128)S(1)} %convolution_add_fusion.1, bf16[8192,512]{1,0:T(8,128)(2,1)S(1)} %bitcast.100, s32[512,256]{1,0:T(8,128)S(1)} %copy-done), kind=kOutput, calls=%fused_computation.2 | convolution fusion | flops 2151809024 | bytes 25690112 | tf_op jit(solution)/shard_map/dot_general | solution.py:82
  357.6 0.0 all-reduce.3.cloned.1.call-update
  357.7 39.2 %all-reduce.3.cloned.1.call-done = f32[8192,256]{1,0:T(8,128)} async-done(((f32[8192,256]{1,0:T(8,128)}), f32[8192,256]{1,0:T(8,128)}) %all-reduce.3.cloned.1.call-update) | async-done | bytes 8388624 | tf_op jit(solution)/shard_map/psum | solution.py:85
  396.9 3.8 fusion.17
  (23 shorter events, 0.0 us)
Async XLA Ops:
  7.6 69.1 %collective-permute-start = (bf16[511,512]{1,0:T(8,128)(2,1)S(1)}, bf16[511,512]{1,0:T(8,128)(2,1)S(1)}, u32[]{:S(2)}, u32[]{:S(2)}) collective-permute-start(bf16[511,512]{1,0:T(8,128)(2,1)S(1)} %slice.73), channel_id=1, source_target_pairs={{2,0},{4,2},{6,4},{8,6},{10,8},{12,10},{14,12},{3,1},{5,3},{7,5},{... | collective-permute-start | bytes 1569800 | tf_op jit(solution)/shard_map/ppermute | solution.py:25
  41.2 7.3 %copy-start.1 = (bf16[512,4606]{1,0:T(8,128)(2,1)S(1)}, bf16[512,4606]{1,0:T(8,128)(2,1)}, u32[]{:S(2)}) copy-start(bf16[512,4606]{1,0:T(8,128)(2,1)} %convert_element_type.50) | copy-start | bytes 14149636
  48.5 12.6 %slice-start.6 = ((s8[33546240]{0:T(1024)(128)(4,1)}), s8[4194304]{0:T(1024)(128)(4,1)S(1)}, s32[]{:S(2)}) async-start(s8[33546240]{0:T(1024)(128)(4,1)} %bitcast.113), calls=%async_computation.8 | async-start | bytes 8388608
  48.5 12.6 %slice-start.7 = ((s8[33546240]{0:T(1024)(128)(4,1)}), s8[4194304]{0:T(1024)(128)(4,1)S(1)}, s32[]{:S(2)}) async-start(s8[33546240]{0:T(1024)(128)(4,1)} %bitcast.113), calls=%async_computation.9 | async-start | bytes 8388608
  48.5 12.6 %slice-start.8 = ((s8[33546240]{0:T(1024)(128)(4,1)}), s8[4194304]{0:T(1024)(128)(4,1)S(1)}, s32[]{:S(2)}) async-start(s8[33546240]{0:T(1024)(128)(4,1)} %bitcast.113), calls=%async_computation.10 | async-start | bytes 8388608
  48.5 12.6 %slice-start.9 = ((s8[33546240]{0:T(1024)(128)(4,1)}), s8[4194304]{0:T(1024)(128)(4,1)S(1)}, s32[]{:S(2)}) async-start(s8[33546240]{0:T(1024)(128)(4,1)} %bitcast.113), calls=%async_computation.11 | async-start | bytes 8388608
  48.5 12.6 %slice-start.10 = ((s8[33546240]{0:T(1024)(128)(4,1)}), s8[4194304]{0:T(1024)(128)(4,1)S(1)}, s32[]{:S(2)}) async-start(s8[33546240]{0:T(1024)(128)(4,1)} %bitcast.113), calls=%async_computation.12 | async-start | bytes 8388608
  54.5 6.6 %slice-start.11 = ((s8[33546240]{0:T(1024)(128)(4,1)}), s8[4194304]{0:T(1024)(128)(4,1)S(1)}, s32[]{:S(2)}) async-start(s8[33546240]{0:T(1024)(128)(4,1)} %bitcast.113), calls=%async_computation.13 | async-start | bytes 8388608
  54.5 6.7 %slice-start.12 = ((s8[33546240]{0:T(1024)(128)(4,1)}), s8[4194304]{0:T(1024)(128)(4,1)S(1)}, s32[]{:S(2)}) async-start(s8[33546240]{0:T(1024)(128)(4,1)} %bitcast.113), calls=%async_computation.14 | async-start | bytes 8388608
  54.5 8.1 %slice-start.13 = ((s8[33546240]{0:T(1024)(128)(4,1)}), s8[4186112]{0:T(1024)(128)(4,1)S(1)}, s32[]{:S(2)}) async-start(s8[33546240]{0:T(1024)(128)(4,1)} %bitcast.113), calls=%async_computation.15 | async-start | bytes 8372224
  97.6 101.4 %all-to-all-start = ((bf16[8,8,64,512]{3,2,1,0:T(8,128)(2,1)}), bf16[8,8,64,512]{3,2,1,0:T(8,128)(2,1)}, u32[]{:S(2)}, u32[]{:S(2)}) async-start(bf16[8,8,64,512]{3,2,1,0:T(8,128)(2,1)} %fusion.106), calls=%async_computation | async-start | bytes 8388608 | tf_op jit(solution)/shard_map/all_to_all | solution.py:18
  106.0 290.9 %all-reduce.3.cloned.1.call-start = ((), (), s32[]{:S(2)}) async-start(), calls=%async_computation.1 | async-start | bytes 16777216 | tf_op jit(solution)/shard_map/psum | solution.py:85
  233.1 11.3 %copy-start = (s32[512,256]{1,0:T(8,128)S(1)}, s32[512,256]{1,0:T(8,128)}, u32[]{:S(2)}) copy-start(s32[512,256]{1,0:T(8,128)} %param.5) | copy-start | bytes 1572868
  242.6 22.9 %collective-permute-start.1 = (bf16[2,64,7,512]{3,1,2,0:T(8,128)(2,1)S(1)}, bf16[2,64,7,512]{3,1,2,0:T(8,128)(2,1)S(1)}, u32[]{:S(2)}, u32[]{:S(2)}) collective-permute-start(bf16[2,64,7,512]{3,1,2,0:T(8,128)(2,1)S(1)} %copy.6), channel_id=1, source_target_pairs={{2,0},{4,2},{6,4},{8,6},{10,8},{12,10},{14,12},{3,1},{5,3},{7,5},{... | collective-permute-start | bytes 2752520 | tf_op jit(solution)/shard_map/ppermute | solution.py:25
  320.1 8.4 %slice-start.4 = ((s8[8388608]{0:T(1024)(128)(4,1)}), s8[4194304]{0:T(1024)(128)(4,1)S(1)}, s32[]{:S(2)}) async-start(s8[8388608]{0:T(1024)(128)(4,1)} %bitcast.107), calls=%async_computation.6 | async-start | bytes 8388608
  320.1 8.4 %slice-start.5 = ((s8[8388608]{0:T(1024)(128)(4,1)}), s8[4194304]{0:T(1024)(128)(4,1)S(1)}, s32[]{:S(2)}) async-start(s8[8388608]{0:T(1024)(128)(4,1)} %bitcast.107), calls=%async_computation.7 | async-start | bytes 8388608
  331.0 6.2 %slice-start.2 = ((s8[8388608]{0:T(1024)(128)(4,1)}), s8[4194304]{0:T(1024)(128)(4,1)S(1)}, s32[]{:S(2)}) async-start(s8[8388608]{0:T(1024)(128)(4,1)} %bitcast.103), calls=%async_computation.4 | async-start | bytes 8388608
  331.0 6.2 %slice-start.3 = ((s8[8388608]{0:T(1024)(128)(4,1)}), s8[4194304]{0:T(1024)(128)(4,1)S(1)}, s32[]{:S(2)}) async-start(s8[8388608]{0:T(1024)(128)(4,1)} %bitcast.103), calls=%async_computation.5 | async-start | bytes 8388608
  345.8 6.2 %slice-start = ((s8[8388608]{0:T(1024)(128)(4,1)}), s8[4194304]{0:T(1024)(128)(4,1)S(1)}, s32[]{:S(2)}) async-start(s8[8388608]{0:T(1024)(128)(4,1)} %bitcast.98), calls=%async_computation.2 | async-start | bytes 8388608
  345.8 6.2 %slice-start.1 = ((s8[8388608]{0:T(1024)(128)(4,1)}), s8[4194304]{0:T(1024)(128)(4,1)S(1)}, s32[]{:S(2)}) async-start(s8[8388608]{0:T(1024)(128)(4,1)} %bitcast.98), calls=%async_computation.3 | async-start | bytes 8388608
Sparse Core Ops, SparseCore 0:
  357.8 39.0 all-reduce.2
